TPU v7x, 32 devices: a whole 2x2x4 slice. The times are simulated.
32 devices in a mesh: dp: 4 (over y, x), shard: 8 (over z, core).
Axes of the slice: x: 2, y: 2, z: 4, core: 2. Of those that a mesh axis runs over, the one named last changes fastest.
Arguments:
- hot_ids: int32 [4096, 8], P(('dp', 'shard')), may hold values from 0 to 4095
- cold_owner: int32 [8192, 1], P(('dp', 'shard')), may hold values from 0 to 7; in each aligned block of 256 rows (0 to 255, 256 to 511, ...) at most 64 rows name the same one
- cold_offset: int32 [8192], P(('dp', 'shard')), may hold values from 0 to 4095
- hot_table: bfloat16 [4096, 128], replicated, may hold values from -2 to 2
- cold_table: bfloat16 [32768, 128], P('shard'), may hold values from -4 to 4
- w_in: bfloat16 [256, 4096], P(None, 'shard'), may hold values from -0.375 to 0.375
- bias_in: bfloat16 [1, 4096], P(None, 'shard'), may hold values from -0.59765625 to 0.59765625
- w_out: bfloat16 [1, 4096], P(None, 'shard'), may hold values from -0.1875 to 0.1875
- cotangent: float32 [4096], P(('dp', 'shard')), may hold values from -10 to 10
Outputs:
- logits: float32 [4096], P(('dp', 'shard'))
- hot_grad: bfloat16 [4096, 128], P('shard')
- cold_grad: bfloat16 [32768, 128], P('shard')
- w_in_grad: float32 [256, 4096], P(None, 'shard')
Inputs may be any that keep to these rules, and one draw needn't show every extreme that they name: `cold_owner`: within the 256 cold lookups of one device no owner is named more than 64 times, a bound that some block reaches.
All inputs are finite; a program needn't handle non-finite values.
Results may differ from a plain program's by a relative error of at most 0.015.
Values may be sent and summed in bfloat16 or wider, within the bound.
A program may use at most 64 MiB of HBM per device.

v0:
```python
import jax
import jax.numpy as jnp
from jax import lax
from jax.sharding import PartitionSpec as P


def contract_rows(left, right):
    return lax.dot_general(
        left, right, (((0,), (0,)), ((), ())), preferred_element_type=jnp.float32
    )


def shards(
    hot_ids, cold_owner, cold_offset, hot_table, cold_table, w_in, bias_in, w_out, cotangent
):
    shard_count = lax.axis_size("shard")
    my_index = lax.axis_index("shard")
    samples_dev = hot_ids.shape[0]
    hot_width = hot_ids.shape[1]
    table_rows = hot_table.shape[0]
    embed = hot_table.shape[1]
    kept_rows = table_rows // shard_count
    owned_rows = cold_table.shape[0]
    row_numbers = jnp.arange(table_rows, dtype=jnp.int32)
    hot_counts = jnp.zeros((samples_dev, table_rows), jnp.float32)
    for lookup in range(hot_width):
        hot_counts = hot_counts + (hot_ids[:, lookup][:, None] == row_numbers[None, :]).astype(
            jnp.float32
        )
    hot_counts = hot_counts.astype(jnp.bfloat16)
    hot_pooled = jnp.dot(hot_counts, hot_table, preferred_element_type=jnp.float32)
    owner_ids = cold_owner[:, 0]
    lookups = owner_ids.shape[0]
    per_sample = lookups // samples_dev
    capacity = max(2, 2 * lookups // shard_count)
    matches = (owner_ids[:, None] == jnp.arange(shard_count, dtype=jnp.int32)[None, :]).astype(
        jnp.int32
    )
    ordinal = jnp.cumsum(matches, axis=0) - 1
    slot_index = jnp.sum(ordinal * matches, axis=1)
    slot_place = owner_ids * capacity + slot_index
    slot_match = slot_place[:, None] == jnp.arange(shard_count * capacity, dtype=jnp.int32)[None, :]
    requests = jnp.sum(jnp.where(slot_match, cold_offset[:, None], 0), axis=0).reshape(
        shard_count, capacity
    )
    present = jnp.sum(slot_match.astype(jnp.int32), axis=0).reshape(shard_count, capacity)
    slot_table = slot_match.astype(jnp.bfloat16)
    offsets = lax.all_to_all(requests, "shard", split_axis=0, concat_axis=0, tiled=True)
    markers = lax.all_to_all(present, "shard", split_axis=0, concat_axis=0, tiled=True)
    fetched = jnp.take(cold_table, offsets, axis=0)
    fetched = jnp.where(markers[:, :, None] > 0, fetched, jnp.zeros_like(fetched))
    answer = lax.all_to_all(fetched, "shard", split_axis=0, concat_axis=0, tiled=True)
    mine = jnp.dot(slot_table, answer.reshape(-1, embed), preferred_element_type=jnp.float32)
    cold_pooled = jnp.sum(mine.reshape(samples_dev, per_sample, embed), axis=1)
    inputs = jnp.concatenate([hot_pooled, cold_pooled], axis=1).astype(jnp.bfloat16)
    group_inputs = lax.all_gather(inputs, "shard", axis=0, tiled=True)
    preact = (
        jnp.dot(group_inputs, w_in, preferred_element_type=jnp.float32)
        + bias_in[0].astype(jnp.float32)[None, :]
    )
    sigma = jax.nn.sigmoid(preact)
    hidden = (preact * sigma).astype(jnp.bfloat16)
    logit_share = jnp.dot(hidden, w_out[0], preferred_element_type=jnp.float32)
    group_logits = lax.psum(logit_share, "shard")
    logits = lax.dynamic_slice_in_dim(group_logits, my_index * samples_dev, samples_dev, 0)
    group_cotangent = lax.all_gather(cotangent, "shard", axis=0, tiled=True)
    slope = sigma * (1.0 + preact * (1.0 - sigma))
    hidden_grad = (group_cotangent[:, None] * w_out[0].astype(jnp.float32)[None, :] * slope).astype(
        jnp.bfloat16
    )
    weight_group = contract_rows(group_inputs, hidden_grad).astype(jnp.bfloat16)
    input_grad = lax.psum_scatter(
        jnp.dot(hidden_grad, w_in.T, preferred_element_type=jnp.float32).astype(jnp.bfloat16),
        "shard",
        scatter_dimension=0,
        tiled=True,
    )
    hot_part = contract_rows(hot_counts, input_grad[:, :embed])
    hot_everywhere = lax.psum(hot_part, ("dp", "shard"))
    hot_total = lax.dynamic_slice_in_dim(hot_everywhere, my_index * kept_rows, kept_rows, 0)
    per_lookup = jnp.repeat(input_grad[:, embed:], per_sample, axis=0)
    outgoing = (
        contract_rows(slot_table, per_lookup)
        .astype(jnp.bfloat16)
        .reshape(shard_count, capacity, embed)
    )
    incoming = lax.all_to_all(outgoing, "shard", split_axis=0, concat_axis=0, tiled=True)
    offset_table = (
        offsets.reshape(-1)[:, None] == jnp.arange(owned_rows, dtype=jnp.int32)[None, :]
    ).astype(jnp.bfloat16)
    cold_part = contract_rows(offset_table, incoming.reshape(-1, embed))
    cold_total, weight_total = (
        lax.psum(cold_part.astype(jnp.bfloat16), "dp").astype(jnp.float32),
        lax.psum(weight_group, "dp").astype(jnp.float32),
    )
    return (logits, hot_total.astype(jnp.bfloat16), cold_total.astype(jnp.bfloat16), weight_total)


def solution(mesh):
    in_specs = (
        P(("dp", "shard"), None),
        P(("dp", "shard"), None),
        P(("dp", "shard")),
        P(),
        P("shard", None),
        P(None, "shard"),
        P(None, "shard"),
        P(None, "shard"),
        P(("dp", "shard")),
    )
    out_specs = (P(("dp", "shard")), P("shard", None), P("shard", None), P(None, "shard"))
    return jax.shard_map(shards, mesh=mesh, in_specs=in_specs, out_specs=out_specs, check_vma=False)
```

profile of v0, /device:TPU:0, one launch (start us, length us, event | category | flops | bytes accessed | tf_op | source)
XLA Modules:
  0.0 214.7 jit_solution(14971163135114629105)
XLA Ops:
  7.2 0.8 fusion.11
  8.8 0.8 fusion.10
  10.1 1.3 fusion.14
  11.4 0.8 convert_reduce_fusion
  12.9 6.3 %all-to-all-start.1 = ((s32[8,1,64]{2,1,0:T(1,128)}), s32[8,1,64]{2,1,0:T(1,128)S(1)}, u32[]{:S(2)}, u32[]{:S(2)}) async-start(s32[8,1,64]{2,1,0:T(1,128)} %all_to_all.24), calls=%async_computation.1 | async-start | bytes 8192 | tf_op jit(solution)/shard_map/all_to_all | solution.py:48
  19.3 1.0 slice_bitcast_fusion.7
  20.2 0.7 reduce.2
  22.5 12.3 %all-gather = f32[8,1,128]{2,1,0:T(1,128)S(1)} all-gather(f32[1,1,128]{2,1,0:T(1,128)} %bitcast.77), channel_id=1, replica_groups=mesh['dp'=4,'shard'=8] {'shard'}, dimensions={0}, use_global_device_ids=true | all-gather | bytes 4608 | tf_op jit(solution)/shard_map/all_gather | solution.py:66
  34.8 3.3 %all-to-all-start = ((s32[8,1,64]{2,1,0:T(1,128)}), s32[8,1,64]{2,1,0:T(1,128)S(1)}, u32[]{:S(2)}, u32[]{:S(2)}) async-start(s32[8,1,64]{2,1,0:T(1,128)} %all_to_all.22), calls=%async_computation | async-start | bytes 8192 | tf_op jit(solution)/shard_map/all_to_all | solution.py:49
  38.3 5.3 %all-to-all-done = s32[8,1,64]{2,1,0:T(1,128)S(1)} async-done(((s32[8,1,64]{2,1,0:T(1,128)}), s32[8,1,64]{2,1,0:T(1,128)S(1)}, u32[]{:S(2)}, u32[]{:S(2)}) %all-to-all-start) | async-done | bytes 2080 | tf_op jit(solution)/shard_map/all_to_all | solution.py:49
  43.6 1.3 gather_fusion
  44.9 0.9 select_select_fusion
  45.8 3.4 %all-to-all-start.2 = ((bf16[8,64,128]{2,1,0:T(8,128)(2,1)}), bf16[8,64,128]{2,1,0:T(8,128)(2,1)S(1)}, u32[]{:S(2)}, u32[]{:S(2)}) async-start(bf16[8,64,128]{2,1,0:T(8,128)(2,1)} %select_select_fusion), calls=%async_computation.2 | async-start | bytes 262144 | tf_op jit(solution)/shard_map/all_to_all | solution.py:52
  49.2 3.7 %convolution_convert_fusion.3 = bf16[128,128]{0,1:T(8,128)(2,1)S(1)} fusion(bf16[4096,128]{1,0:T(8,128)(2,1)} %param.12, s32[128]{0:T(128)S(1)} %get-tuple-element.16, s32[128]{0:T(128)S(1)} %get-tuple-element.17, s32[128]{0:T(128)S(1)} %get-tuple-element.11, s32[128]{0:T(128)S(1)} %get-tuple-element.12, s32[128]{0:T(128)S(1)} %get-tuple-element.13, ...), kind=kOutput, calls=%fused_computation.21 | convolution fusion | flops 146817024 | bytes 1085440 | tf_op jit(solution)/shard_map/dot_general | solution.py:31
  53.0 2.9 %all-to-all-done.2 = bf16[8,64,128]{2,1,0:T(8,128)(2,1)S(1)} async-done(((bf16[8,64,128]{2,1,0:T(8,128)(2,1)}), bf16[8,64,128]{2,1,0:T(8,128)(2,1)S(1)}, u32[]{:S(2)}, u32[]{:S(2)}) %all-to-all-start.2) | async-done | bytes 131104 | tf_op jit(solution)/shard_map/all_to_all | solution.py:52
  56.3 14.0 %all_gather.6 = bf16[1024,256]{0,1:T(8,128)(2,1)S(1)} all-gather(bf16[128,256]{0,1:T(8,128)(2,1)S(1)} %pad_maximum_fusion), channel_id=1, replica_groups=mesh['dp'=4,'shard'=8] {'shard'}, dimensions={0}, use_global_device_ids=true | all-gather | bytes 589824 | tf_op jit(solution)/shard_map/all_gather | solution.py:56
  70.3 2.3 %multiply_convert_fusion = (bf16[1024,512]{1,0:T(8,128)(2,1)S(1)}, f32[1024,512]{1,0:T(8,128)}) fusion(f32[512]{0:T(512)S(1)} %mul.50, f32[1024]{0:T(1024)S(1)} %bitcast.70, f32[512]{0:T(512)S(1)} %bitcast.75, bf16[1024,256]{0,1:T(8,128)(2,1)S(1)} %all_gather.6, bf16[256,512]{1,0:T(8,128)(2,1)S(1)} %copy-done.1), kind=kOutput, calls=%fused_computation.5 | convolution fusion | flops 274202624 | bytes 3940352 | tf_op jit(solution)/shard_map/dot_general | solution.py:58
  72.6 1.3 convolution_convert_fusion
  74.6 28.9 %reduce-scatter.2.cloned.1.call-done = bf16[128,256]{1,0:T(8,128)(2,1)} async-done(((bf16[1024,256]{1,0:T(8,128)(2,1)}), bf16[128,256]{1,0:T(8,128)(2,1)}) %reduce-scatter.2.cloned.1.call-update) | async-done | bytes 65552 | tf_op jit(solution)/shard_map/reduce_scatter | solution.py:72
  103.5 0.8 slice.52
  104.3 1.1 convolution_convert_fusion.2
  105.4 3.4 %all-to-all-start.3 = ((bf16[8,64,128]{2,1,0:T(8,128)(2,1)}), bf16[8,64,128]{2,1,0:T(8,128)(2,1)S(1)}, u32[]{:S(2)}, u32[]{:S(2)}) async-start(bf16[8,64,128]{2,1,0:T(8,128)(2,1)} %bitcast.27), calls=%async_computation.4 | async-start | bytes 262144 | tf_op jit(solution)/shard_map/all_to_all | solution.py:87
  108.8 1.2 convolution_convert_fusion.1
  110.0 5.5 %all-to-all-done.3 = bf16[8,64,128]{2,1,0:T(8,128)(2,1)S(1)} async-done(((bf16[8,64,128]{2,1,0:T(8,128)(2,1)}), bf16[8,64,128]{2,1,0:T(8,128)(2,1)S(1)}, u32[]{:S(2)}, u32[]{:S(2)}) %all-to-all-start.3) | async-done | bytes 131104 | tf_op jit(solution)/shard_map/all_to_all | solution.py:87
  115.5 3.4 %fusion.1 = bf16[4096,128]{1,0:T(8,128)(2,1)} fusion(bf16[512,128]{1,0:T(8,128)(2,1)S(1)} %bitcast.62, s32[512]{0:T(512)S(1)} %eq.248), kind=kOutput, calls=%fused_computation.3 | convolution fusion | flops 539492352 | bytes 1181696 | tf_op jit(solution)/shard_map/dot_general | solution.py:8
  118.9 2.3 %fusion.3 = f32[1,1024]{1,0:T(1,128)S(1)} fusion(f32[1024,512]{1,0:T(8,128)} %get-tuple-element.19, f32[512]{0:T(512)S(1)} %bitcast.76, bf16[1,512]{1,0:T(2,128)(2,1)S(1)} %copy-done.3), kind=kOutput, calls=%fused_computation.22 | convolution fusion | flops 4194304 | bytes 2104320 | tf_op jit(solution)/shard_map/dot_general | solution.py:63
  121.2 14.4 %psum.28 = f32[1024]{0:T(1024)S(1)} all-reduce(f32[1024]{0:T(1024)S(1)} %bitcast.71), channel_id=1, replica_groups=mesh['dp'=4,'shard'=8] {'shard'}, use_global_device_ids=true, to_apply=%region_6.7 | all-reduce | flops 1024 | bytes 8192 | tf_op jit(solution)/shard_map/psum | solution.py:64
  136.2 2.3 %fusion.6 = f32[4096,128]{1,0:T(8,128)S(1)} fusion(s32[128]{0:T(128)S(1)} %get-tuple-element.16, s32[128]{0:T(128)S(1)} %get-tuple-element.17, s32[128]{0:T(128)S(1)} %get-tuple-element.11, s32[128]{0:T(128)S(1)} %get-tuple-element.12, s32[128]{0:T(128)S(1)} %get-tuple-element.13, s32[128]{0:T(128)S(1)} %get-tuple-element.14, ...), kind=kOutput, calls=%fused_computation.28 | convolution fusion | flops 146800640 | bytes 2134016 | tf_op jit(solution)/shard_map/dot_general | solution.py:8
  138.6 63.7 %all-reduce.5 = bf16[4096,128]{1,0:T(8,128)(2,1)} all-reduce(f32[4096,128]{1,0:T(8,128)S(1)} %fusion.6), channel_id=1, replica_groups=mesh['dp'=4,'shard'=8] {'dp','shard'}, use_global_device_ids=true, to_apply=%region_8.9 | all-reduce | flops 524288 | bytes 3145728 | tf_op jit(solution)/shard_map/psum | solution.py:79
  202.3 1.6 dynamic-slice_convert_fusion
  203.8 1.8 convert_element_type.86
  205.6 2.3 %copy.27 = bf16[4096,128]{1,0:T(8,128)(2,1)} copy(bf16[4096,128]{1,0:T(8,128)(2,1)} %get-tuple-element.22) | data formatting | bytes 2097152
  (37 shorter events, 5.6 us)
Async XLA Ops:
  7.2 36.4 %copy-start = (bf16[4096,128]{1,0:T(8,128)(2,1)S(1)}, bf16[4096,128]{1,0:T(8,128)(2,1)}, u32[]{:S(2)}) copy-start(bf16[4096,128]{1,0:T(8,128)(2,1)} %param.13) | copy-start | bytes 3145732
  12.9 21.9 %all-to-all-start.1 = ((s32[8,1,64]{2,1,0:T(1,128)}), s32[8,1,64]{2,1,0:T(1,128)S(1)}, u32[]{:S(2)}, u32[]{:S(2)}) async-start(s32[8,1,64]{2,1,0:T(1,128)} %all_to_all.24), calls=%async_computation.1 | async-start | bytes 8192 | tf_op jit(solution)/shard_map/all_to_all | solution.py:48
  34.8 8.7 %all-to-all-start = ((s32[8,1,64]{2,1,0:T(1,128)}), s32[8,1,64]{2,1,0:T(1,128)S(1)}, u32[]{:S(2)}, u32[]{:S(2)}) async-start(s32[8,1,64]{2,1,0:T(1,128)} %all_to_all.22), calls=%async_computation | async-start | bytes 8192 | tf_op jit(solution)/shard_map/all_to_all | solution.py:49
  45.8 10.1 %all-to-all-start.2 = ((bf16[8,64,128]{2,1,0:T(8,128)(2,1)}), bf16[8,64,128]{2,1,0:T(8,128)(2,1)S(1)}, u32[]{:S(2)}, u32[]{:S(2)}) async-start(bf16[8,64,128]{2,1,0:T(8,128)(2,1)} %select_select_fusion), calls=%async_computation.2 | async-start | bytes 262144 | tf_op jit(solution)/shard_map/all_to_all | solution.py:52
  49.2 54.3 %reduce-scatter.2.cloned.1.call-start = ((), (), s32[]{:S(2)}) async-start(), calls=%async_computation.5 | async-start | bytes 589824 | tf_op jit(solution)/shard_map/reduce_scatter | solution.py:72
  49.2 21.1 %copy-start.1 = (bf16[256,512]{1,0:T(8,128)(2,1)S(1)}, bf16[256,512]{1,0:T(8,128)(2,1)}, u32[]{:S(2)}) copy-start(bf16[256,512]{1,0:T(8,128)(2,1)} %param.14) | copy-start | bytes 786436
  105.4 10.1 %all-to-all-start.3 = ((bf16[8,64,128]{2,1,0:T(8,128)(2,1)}), bf16[8,64,128]{2,1,0:T(8,128)(2,1)S(1)}, u32[]{:S(2)}, u32[]{:S(2)}) async-start(bf16[8,64,128]{2,1,0:T(8,128)(2,1)} %bitcast.27), calls=%async_computation.4 | async-start | bytes 262144 | tf_op jit(solution)/shard_map/all_to_all | solution.py:87
  108.8 95.1 %all-reduce.4.cloned.1.call-start = ((), (), s32[]{:S(2)}) async-start(), calls=%async_computation.6 | async-start | bytes 2621440 | tf_op jit(solution)/shard_map/psum | solution.py:93
  115.5 3.4 %copy-start.3 = (bf16[1,512]{1,0:T(2,128)(2,1)S(1)}, bf16[1,512]{1,0:T(2,128)(2,1)}, u32[]{:S(2)}) copy-start(bf16[1,512]{1,0:T(2,128)(2,1)} %param.16) | copy-start | bytes 3076
  118.9 17.3 %copy-start.2 = (bf16[128,256]{1,0:T(8,128)(2,1)S(1)}, bf16[128,256]{1,0:T(8,128)(2,1)}, u32[]{:S(2)}) copy-start(bf16[128,256]{1,0:T(8,128)(2,1)} %reduce-scatter.2.cloned.1.call-done) | copy-start | bytes 196612
Sparse Core Ops, SparseCore 0:
  74.0 29.4 reduce-scatter.1
  119.0 61.0 all-reduce.3
where the time goes:
time: 216 us; the launch traced here: 215 us
  blocking collectives  104 us (48%)
  waiting for transfers between devices  42.6 us (20%)
  matrix products  17.9 us (8%)
  starting transfers between devices  16.5 us (8%)
  between operations  14.2 us (7%)
  local copies, waits for them, and re-layouts  10.1 us (5%)
  other arithmetic  9.09 us (4%)
    psum x1, blocking collectives, shards(): hot_everywhere = lax.psum(hot_part, ('dp', 'shard'))  63.7 us
    reduce_scatter x1, waiting for transfers between devices, shards(): lax.psum_scatter(jnp.dot(hidden_grad, w_in.T, preferred_element_type=jnp....  28.9 us
    psum x1, blocking collectives, shards(): group_logits = lax.psum(logit_share, 'shard')  14.4 us
    all_gather x1, blocking collectives, shards(): group_inputs = lax.all_gather(inputs, 'shard', axis=0, tiled=True)  14 us
    all_gather x1, blocking collectives, shards(): group_cotangent = lax.all_gather(cotangent, 'shard', axis=0, tiled=True)  12.3 us
    dot_general x4, matrix products, contract_rows(): lax.dot_general(left, right, (((0,), (0,)), ((), ())), preferred_element_...  8.01 us
    all_to_all x1, starting transfers between devices, shards(): lax.all_to_all(requests, 'shard', split_axis=0, concat_axis=0, tiled=True)  6.33 us
    all_to_all x1, waiting for transfers between devices, shards(): lax.all_to_all(outgoing, 'shard', split_axis=0, concat_axis=0, tiled=True)  5.5 us
  transfers between devices with their start and end apart: 6, of which 4 were waited for; matrix products, arithmetic and copies ran while one was open for 7% of the time, Pallas kernels for 0%

commit v1 on v0

--- a/solution.py
+++ b/solution.py
@@ -76,7 +76,9 @@
         tiled=True,
     )
     hot_part = contract_rows(hot_counts, input_grad[:, :embed])
-    hot_everywhere = lax.psum(hot_part, ("dp", "shard"))
+    hot_everywhere = hot_part
+    for over in ("shard", "dp"):
+        hot_everywhere = lax.psum(hot_everywhere, over)
     hot_total = lax.dynamic_slice_in_dim(hot_everywhere, my_index * kept_rows, kept_rows, 0)
     per_lookup = jnp.repeat(input_grad[:, embed:], per_sample, axis=0)
     outgoing = (

time: 216 us -> 280 us (1.30)
  waiting for transfers between devices: 42.6 us -> 75.4 us
  blocking collectives: 104 us -> 135 us
    psum x0 -> x1, waiting for transfers between devices: none -> 30.7 us  [shards(): hot_everywhere = lax.psum(hot_everywhere, over)]
    psum x1, blocking collectives: 63.7 us -> 94.2 us  [shards(): hot_everywhere = lax.psum(hot_everywhere, over)]
  transfers between devices with their start and end apart: 6 -> 7, of which waited for: 4 -> 5; matrix products, arithmetic and copies ran while one was open for 7% -> 6% of each run, Pallas kernels for 0% -> 0%
where the time goes in v1:
time: 280 us; the launch traced here: 279 us
  blocking collectives  135 us (48%)
  waiting for transfers between devices  75.4 us (27%)
  matrix products  19.9 us (7%)
  starting transfers between devices  16.7 us (6%)
  between operations  13.9 us (5%)
  other arithmetic  9.09 us (3%)
  local copies, waits for them, and re-layouts  8.44 us (3%)
    psum x1, blocking collectives, shards(): hot_everywhere = lax.psum(hot_everywhere, over)  94.2 us
    psum x1, waiting for transfers between devices, shards(): hot_everywhere = lax.psum(hot_everywhere, over)  30.7 us
    reduce_scatter x1, waiting for transfers between devices, shards(): lax.psum_scatter(jnp.dot(hidden_grad, w_in.T, preferred_element_type=jnp....  29.6 us
    psum x1, blocking collectives, shards(): group_logits = lax.psum(logit_share, 'shard')  14.8 us
    all_gather x1, blocking collectives, shards(): group_inputs = lax.all_gather(inputs, 'shard', axis=0, tiled=True)  14 us
    all_gather x1, blocking collectives, shards(): group_cotangent = lax.all_gather(cotangent, 'shard', axis=0, tiled=True)  12.3 us
    dot_general x4, matrix products, contract_rows(): lax.dot_general(left, right, (((0,), (0,)), ((), ())), preferred_element_...  10.1 us
    all_to_all x1, waiting for transfers between devices, shards(): lax.all_to_all(outgoing, 'shard', split_axis=0, concat_axis=0, tiled=True)  6.9 us
  transfers between devices with their start and end apart: 7, of which 5 were waited for; matrix products, arithmetic and copies ran while one was open for 6% of the time, Pallas kernels for 0%

profile of v1, /device:TPU:0, one launch (start us, length us, event | category | flops | bytes accessed | tf_op | source)
XLA Modules:
  0.0 278.6 jit_solution(12758000550311607130)
XLA Ops:
  7.2 0.8 fusion.11
  8.8 0.8 fusion.10
  10.1 1.3 fusion.14
  11.4 0.8 convert_reduce_fusion
  12.9 6.3 %all-to-all-start.1 = ((s32[8,1,64]{2,1,0:T(1,128)}), s32[8,1,64]{2,1,0:T(1,128)S(1)}, u32[]{:S(2)}, u32[]{:S(2)}) async-start(s32[8,1,64]{2,1,0:T(1,128)} %all_to_all.24), calls=%async_computation.1 | async-start | bytes 8192 | tf_op jit(solution)/shard_map/all_to_all | solution.py:48
  19.3 1.0 slice_bitcast_fusion.7
  20.2 0.7 reduce.2
  20.9 0.7 add.106
  22.5 12.3 %all-gather = f32[8,1,128]{2,1,0:T(1,128)S(1)} all-gather(f32[1,1,128]{2,1,0:T(1,128)} %bitcast.77), channel_id=1, replica_groups=mesh['dp'=4,'shard'=8] {'shard'}, dimensions={0}, use_global_device_ids=true | all-gather | bytes 4608 | tf_op jit(solution)/shard_map/all_gather | solution.py:66
  34.8 3.3 %all-to-all-start = ((s32[8,1,64]{2,1,0:T(1,128)}), s32[8,1,64]{2,1,0:T(1,128)S(1)}, u32[]{:S(2)}, u32[]{:S(2)}) async-start(s32[8,1,64]{2,1,0:T(1,128)} %all_to_all.22), calls=%async_computation | async-start | bytes 8192 | tf_op jit(solution)/shard_map/all_to_all | solution.py:49
  38.3 5.3 %all-to-all-done = s32[8,1,64]{2,1,0:T(1,128)S(1)} async-done(((s32[8,1,64]{2,1,0:T(1,128)}), s32[8,1,64]{2,1,0:T(1,128)S(1)}, u32[]{:S(2)}, u32[]{:S(2)}) %all-to-all-start) | async-done | bytes 2080 | tf_op jit(solution)/shard_map/all_to_all | solution.py:49
  43.6 1.3 gather_fusion
  44.9 0.9 select_select_fusion
  45.8 3.4 %all-to-all-start.2 = ((bf16[8,64,128]{2,1,0:T(8,128)(2,1)}), bf16[8,64,128]{2,1,0:T(8,128)(2,1)S(1)}, u32[]{:S(2)}, u32[]{:S(2)}) async-start(bf16[8,64,128]{2,1,0:T(8,128)(2,1)} %select_select_fusion), calls=%async_computation.2 | async-start | bytes 262144 | tf_op jit(solution)/shard_map/all_to_all | solution.py:52
  49.2 3.7 %convolution_convert_fusion.3 = bf16[128,128]{0,1:T(8,128)(2,1)S(1)} fusion(bf16[4096,128]{1,0:T(8,128)(2,1)} %param.12, s32[128]{0:T(128)S(1)} %get-tuple-element.16, s32[128]{0:T(128)S(1)} %get-tuple-element.17, s32[128]{0:T(128)S(1)} %get-tuple-element.11, s32[128]{0:T(128)S(1)} %get-tuple-element.12, s32[128]{0:T(128)S(1)} %get-tuple-element.13, ...), kind=kOutput, calls=%fused_computation.21 | convolution fusion | flops 146817024 | bytes 1085440 | tf_op jit(solution)/shard_map/dot_general | solution.py:31
  53.0 2.9 %all-to-all-done.2 = bf16[8,64,128]{2,1,0:T(8,128)(2,1)S(1)} async-done(((bf16[8,64,128]{2,1,0:T(8,128)(2,1)}), bf16[8,64,128]{2,1,0:T(8,128)(2,1)S(1)}, u32[]{:S(2)}, u32[]{:S(2)}) %all-to-all-start.2) | async-done | bytes 131104 | tf_op jit(solution)/shard_map/all_to_all | solution.py:52
  56.3 14.0 %all_gather.6 = bf16[1024,256]{0,1:T(8,128)(2,1)S(1)} all-gather(bf16[128,256]{0,1:T(8,128)(2,1)S(1)} %pad_maximum_fusion), channel_id=1, replica_groups=mesh['dp'=4,'shard'=8] {'shard'}, dimensions={0}, use_global_device_ids=true | all-gather | bytes 589824 | tf_op jit(solution)/shard_map/all_gather | solution.py:56
  70.3 2.3 multiply_convert_fusion
  72.6 1.3 convolution_convert_fusion
  73.9 29.6 %reduce-scatter.2.cloned.1.call-done = bf16[128,256]{1,0:T(8,128)(2,1)} async-done(((bf16[1024,256]{1,0:T(8,128)(2,1)}), bf16[128,256]{1,0:T(8,128)(2,1)}) %reduce-scatter.2.cloned.1.call-update) | async-done | bytes 65552 | tf_op jit(solution)/shard_map/reduce_scatter | solution.py:72
  103.5 4.4 %fusion.6 = f32[4096,128]{1,0:T(8,128)} fusion(s32[128]{0:T(128)S(1)} %get-tuple-element.16, s32[128]{0:T(128)S(1)} %get-tuple-element.17, s32[128]{0:T(128)S(1)} %get-tuple-element.11, s32[128]{0:T(128)S(1)} %get-tuple-element.12, s32[128]{0:T(128)S(1)} %get-tuple-element.13, s32[128]{0:T(128)S(1)} %get-tuple-element.14, s32[128]{0:T(128)S(1)} %get-tuple-element.15, ...), kind=kOutput, calls=%fused_computation.28 | convolution fusion | flops 146800640 | bytes 2134016 | tf_op jit(solution)/shard_map/dot_general | solution.py:8
  108.7 1.1 convolution_convert_fusion.2
  109.8 3.4 %all-to-all-start.3 = ((bf16[8,64,128]{2,1,0:T(8,128)(2,1)}), bf16[8,64,128]{2,1,0:T(8,128)(2,1)S(1)}, u32[]{:S(2)}, u32[]{:S(2)}) async-start(bf16[8,64,128]{2,1,0:T(8,128)(2,1)} %bitcast.27), calls=%async_computation.4 | async-start | bytes 262144 | tf_op jit(solution)/shard_map/all_to_all | solution.py:89
  113.4 1.1 convolution_convert_fusion.1
  114.5 6.9 %all-to-all-done.3 = bf16[8,64,128]{2,1,0:T(8,128)(2,1)S(1)} async-done(((bf16[8,64,128]{2,1,0:T(8,128)(2,1)}), bf16[8,64,128]{2,1,0:T(8,128)(2,1)S(1)}, u32[]{:S(2)}, u32[]{:S(2)}) %all-to-all-start.3) | async-done | bytes 131104 | tf_op jit(solution)/shard_map/all_to_all | solution.py:89
  121.4 3.4 %fusion.1 = bf16[4096,128]{1,0:T(8,128)(2,1)} fusion(bf16[512,128]{1,0:T(8,128)(2,1)S(1)} %bitcast.62, s32[512]{0:T(512)S(1)} %eq.248), kind=kOutput, calls=%fused_computation.3 | convolution fusion | flops 539492352 | bytes 1181696 | tf_op jit(solution)/shard_map/dot_general | solution.py:8
  124.9 2.3 fusion.3
  127.2 14.8 %psum.35 = f32[1024]{0:T(1024)S(1)} all-reduce(f32[1024]{0:T(1024)S(1)} %bitcast.71), channel_id=1, replica_groups=mesh['dp'=4,'shard'=8] {'shard'}, use_global_device_ids=true, to_apply=%region_6.7 | all-reduce | flops 1024 | bytes 8192 | tf_op jit(solution)/shard_map/psum | solution.py:64
  142.5 30.7 %all-reduce.5.cloned.1.call-done = f32[4096,128]{1,0:T(8,128)} async-done(((f32[4096,128]{1,0:T(8,128)}), f32[4096,128]{1,0:T(8,128)}) %all-reduce.5.cloned.1.call-update) | async-done | bytes 2097168 | tf_op jit(solution)/shard_map/psum | solution.py:81
  173.2 94.2 %all-reduce.8 = bf16[4096,128]{1,0:T(8,128)(2,1)S(1)} all-reduce(f32[4096,128]{1,0:T(8,128)} %all-reduce.5.cloned.1.call-done), channel_id=1, replica_groups=mesh['dp'=4,'shard'=8] {'dp'}, use_global_device_ids=true, to_apply=%region_9.10 | all-reduce | flops 524288 | bytes 3145728 | tf_op jit(solution)/shard_map/psum | solution.py:81
  268.1 1.8 convert_element_type.86
  269.9 2.3 copy.28
  (39 shorter events, 5.8 us)
Async XLA Ops:
  7.2 36.4 %copy-start = (bf16[4096,128]{1,0:T(8,128)(2,1)S(1)}, bf16[4096,128]{1,0:T(8,128)(2,1)}, u32[]{:S(2)}) copy-start(bf16[4096,128]{1,0:T(8,128)(2,1)} %param.13) | copy-start | bytes 3145732
  12.9 21.9 %all-to-all-start.1 = ((s32[8,1,64]{2,1,0:T(1,128)}), s32[8,1,64]{2,1,0:T(1,128)S(1)}, u32[]{:S(2)}, u32[]{:S(2)}) async-start(s32[8,1,64]{2,1,0:T(1,128)} %all_to_all.24), calls=%async_computation.1 | async-start | bytes 8192 | tf_op jit(solution)/shard_map/all_to_all | solution.py:48
  34.8 8.7 %all-to-all-start = ((s32[8,1,64]{2,1,0:T(1,128)}), s32[8,1,64]{2,1,0:T(1,128)S(1)}, u32[]{:S(2)}, u32[]{:S(2)}) async-start(s32[8,1,64]{2,1,0:T(1,128)} %all_to_all.22), calls=%async_computation | async-start | bytes 8192 | tf_op jit(solution)/shard_map/all_to_all | solution.py:49
  45.8 10.1 %all-to-all-start.2 = ((bf16[8,64,128]{2,1,0:T(8,128)(2,1)}), bf16[8,64,128]{2,1,0:T(8,128)(2,1)S(1)}, u32[]{:S(2)}, u32[]{:S(2)}) async-start(bf16[8,64,128]{2,1,0:T(8,128)(2,1)} %select_select_fusion), calls=%async_computation.2 | async-start | bytes 262144 | tf_op jit(solution)/shard_map/all_to_all | solution.py:52
  49.2 54.3 %reduce-scatter.2.cloned.1.call-start = ((), (), s32[]{:S(2)}) async-start(), calls=%async_computation.5 | async-start | bytes 589824 | tf_op jit(solution)/shard_map/reduce_scatter | solution.py:72
  49.2 21.1 %copy-start.1 = (bf16[256,512]{1,0:T(8,128)(2,1)S(1)}, bf16[256,512]{1,0:T(8,128)(2,1)}, u32[]{:S(2)}) copy-start(bf16[256,512]{1,0:T(8,128)(2,1)} %param.14) | copy-start | bytes 786436
  73.8 99.3 %all-reduce.5.cloned.1.call-start = ((), (), s32[]{:S(2)}) async-start(), calls=%async_computation.6 | async-start | bytes 4194304 | tf_op jit(solution)/shard_map/psum | solution.py:81
  107.9 0.8 slice-start
  109.8 11.7 %all-to-all-start.3 = ((bf16[8,64,128]{2,1,0:T(8,128)(2,1)}), bf16[8,64,128]{2,1,0:T(8,128)(2,1)S(1)}, u32[]{:S(2)}, u32[]{:S(2)}) async-start(bf16[8,64,128]{2,1,0:T(8,128)(2,1)} %bitcast.27), calls=%async_computation.4 | async-start | bytes 262144 | tf_op jit(solution)/shard_map/all_to_all | solution.py:89
  113.2 154.9 %all-reduce.7.cloned.1.call-start = ((), (), s32[]{:S(2)}) async-start(), calls=%async_computation.7 | async-start | bytes 2621440 | tf_op jit(solution)/shard_map/psum | solution.py:95
  121.4 3.4 %copy-start.2 = (bf16[1,512]{1,0:T(2,128)(2,1)S(1)}, bf16[1,512]{1,0:T(2,128)(2,1)}, u32[]{:S(2)}) copy-start(bf16[1,512]{1,0:T(2,128)(2,1)} %param.16) | copy-start | bytes 3076
Sparse Core Ops, SparseCore 0:
  74.0 29.4 reduce-scatter.1
  108.0 65.1 all-reduce.4
  177.2 77.7 all-reduce.6
